TPU v7x, 32 devices: a whole 2x2x4 slice. The times are simulated.
32 devices in a mesh: groups: 1, wide: 32 (over z, y, x, core).
Axes of the slice: x: 2, y: 2, z: 4, core: 2. Of those that a mesh axis runs over, the one named last changes fastest.
Arguments:
- trial_bands: bfloat16 [1, 2, 3, 192, 192, 192], P('groups', None, None, 'wide'), may hold values from -160 to 160, as said below
- locked_bands: bfloat16 [4, 2, 3, 192, 192, 192], P('groups', None, None, 'wide'), may hold values from -240 to 240, as said below
- inv_diag: float32 [3, 192, 192, 192], P('groups', None, 'wide'), may hold values from 0.1 to 1
- inv_corr: float32 [3, 192, 192, 192], P('groups', None, 'wide'), may hold values from -0.3 to 0.3
Outputs:
- applied: bfloat16 [1, 2, 3, 192, 192, 192], P('groups', None, None, 'wide')
- rayleigh: float32 [2, 1, 1], P('groups')
Inputs may be any that keep to these rules, and one draw needn't show every extreme that they name: `trial_bands`: sums of locked and independent fields, bounded. `locked_bands`: the locked bands are linearly independent.
All inputs are finite; a program needn't handle non-finite values.
Results may differ from a plain program's by a relative error of at most 0.0013.
Values sent between devices are 32-bit elements; how exact they have to be, the bound alone decides.
A program may use at most 128 MiB of HBM per device.

v0:
```python
import math

import jax
import jax.numpy as jnp
from jax import lax
from jax.sharding import PartitionSpec as P

highest = lax.Precision.HIGHEST


def signed_wave(indices, length):
    shifted = jnp.where(indices < length // 2, indices, indices - length)
    return shifted.astype(jnp.float32) / (length / 2.0)


def cross_wave(wave_x, wave_y, wave_z, vectors):
    comp_x = vectors[..., 0, :, :, :]
    comp_y = vectors[..., 1, :, :, :]
    comp_z = vectors[..., 2, :, :, :]
    along_x = wave_x[:, None, None]
    along_y = wave_y[None, :, None]
    along_z = wave_z[None, None, :]
    return jnp.stack(
        [
            along_y * comp_z - along_z * comp_y,
            along_z * comp_x - along_x * comp_z,
            along_x * comp_y - along_y * comp_x,
        ],
        axis=-4,
    )


def curl_times_i(waves, stacked):
    wave_x, wave_y, wave_z = waves
    return jnp.stack(
        [
            -cross_wave(wave_x, wave_y, wave_z, stacked[1]),
            cross_wave(wave_x, wave_y, wave_z, stacked[0]),
        ],
        axis=0,
    )


def apply_tensor(vectors, inv_diag, inv_corr):
    coupling_xy = inv_corr[0] * jnp.sqrt(inv_diag[0] * inv_diag[1])
    coupling_xz = inv_corr[1] * jnp.sqrt(inv_diag[0] * inv_diag[2])
    coupling_yz = inv_corr[2] * jnp.sqrt(inv_diag[1] * inv_diag[2])
    comp_x = vectors[..., 0, :, :, :]
    comp_y = vectors[..., 1, :, :, :]
    comp_z = vectors[..., 2, :, :, :]
    out_x = inv_diag[0] * comp_x + coupling_xy * comp_y + coupling_xz * comp_z
    out_y = coupling_xy * comp_x + inv_diag[1] * comp_y + coupling_yz * comp_z
    out_z = coupling_xz * comp_x + coupling_yz * comp_y + inv_diag[2] * comp_z
    return jnp.stack([out_x, out_y, out_z], axis=-4)


def complex_table(length, orient):
    indices = jnp.arange(length, dtype=jnp.int32)
    phases = indices[:, None] * indices[None, :] % length
    angles = phases.astype(jnp.float32) * (2.0 * math.pi / length)
    norm_factor = 1.0 / math.sqrt(length)
    cos_table = jnp.cos(angles) * norm_factor
    sin_table = jnp.sin(angles) * norm_factor * orient
    return jnp.stack(
        [jnp.stack([cos_table, sin_table], axis=0), jnp.stack([-sin_table, cos_table], axis=0)],
        axis=0,
    )


def transform(stacked, axis_dim, orient):
    table = complex_table(stacked.shape[axis_dim + 1], orient)
    if axis_dim == 2:
        return jnp.einsum("pbckyz,pqkn->qbcnyz", stacked, table, precision=highest)
    if axis_dim == 3:
        return jnp.einsum("pbcxkz,pqkn->qbcxnz", stacked, table, precision=highest)
    return jnp.einsum("pbcxyk,pqkn->qbcxyn", stacked, table, precision=highest)


def inner_sum(left_rows, right_rows):
    return jnp.einsum("an,bn->ab", left_rows, right_rows, preferred_element_type=jnp.float32)


def remove_locked(gram_sums, trial_re, trial_im, locked_re, locked_im):
    gram_a, gram_q, proj_re, proj_im = gram_sums
    kept_count = gram_a.shape[0]
    gram = jnp.concatenate(
        [jnp.concatenate([gram_a, gram_q], axis=1), jnp.concatenate([gram_q.T, gram_a], axis=1)],
        axis=0,
    )
    rhs_both = jnp.concatenate([proj_re, proj_im], axis=0)
    lower = jnp.linalg.cholesky(gram)
    middle = lax.linalg.triangular_solve(lower, rhs_both, left_side=True, lower=True)
    coef = lax.linalg.triangular_solve(lower, middle, left_side=True, lower=True, transpose_a=True)
    coef_one = coef[:kept_count]
    coef_two = coef[kept_count:]
    locked_re32 = locked_re.astype(jnp.float32)
    locked_im32 = locked_im.astype(jnp.float32)
    out_re = (
        trial_re.astype(jnp.float32)
        - jnp.einsum("ab,an->bn", coef_one, locked_re32, precision=highest)
        + jnp.einsum("ab,an->bn", coef_two, locked_im32, precision=highest)
    )
    out_im = (
        trial_im.astype(jnp.float32)
        - jnp.einsum("ab,an->bn", coef_one, locked_im32, precision=highest)
        - jnp.einsum("ab,an->bn", coef_two, locked_re32, precision=highest)
    )
    return (out_re, out_im)


def maxwell_pass(spectrum, waves, inv_diag, inv_corr, to_space_fn, to_spectrum_fn):
    curled = curl_times_i(waves, spectrum)
    curled = transform(curled, 4, 1.0)
    curled = transform(curled, 3, 1.0)
    moved = to_space_fn(curled)
    space = transform(moved, 2, 1.0)
    weighted = apply_tensor(space, inv_diag, inv_corr)
    front = transform(weighted, 2, -1.0)
    home = to_spectrum_fn(front)
    home = transform(home, 3, -1.0)
    home = transform(home, 4, -1.0)
    return (curl_times_i(waves, home), space, weighted)


def per_device(trial_bands, locked_bands, inv_diag, inv_corr):
    band_count = trial_bands.shape[0]
    kept_count = locked_bands.shape[0]
    local_x = trial_bands.shape[3]
    grid_len = trial_bands.shape[4]
    trial_re = trial_bands[:, 0].reshape(band_count, -1)
    trial_im = trial_bands[:, 1].reshape(band_count, -1)
    locked_re = locked_bands[:, 0].reshape(kept_count, -1)
    locked_im = locked_bands[:, 1].reshape(kept_count, -1)
    gram_a = inner_sum(locked_re, locked_re) + inner_sum(locked_im, locked_im)
    gram_q = inner_sum(locked_im, locked_re) - inner_sum(locked_re, locked_im)
    proj_re = inner_sum(locked_re, trial_re) + inner_sum(locked_im, trial_im)
    proj_im = inner_sum(locked_re, trial_im) - inner_sum(locked_im, trial_re)
    gram_sums = lax.psum((gram_a, gram_q, proj_re, proj_im), "wide")
    flat_re, flat_im = remove_locked(gram_sums, trial_re, trial_im, locked_re, locked_im)
    shape_local = (band_count, 3, local_x, grid_len, grid_len)
    spectrum = jnp.stack([flat_re.reshape(shape_local), flat_im.reshape(shape_local)], axis=0)
    start_x = lax.axis_index("wide") * local_x
    full_axis = jnp.arange(grid_len, dtype=jnp.int32)
    wave_x = signed_wave(start_x + jnp.arange(local_x, dtype=jnp.int32), grid_len)
    wave_full = signed_wave(full_axis, grid_len)
    waves = (wave_x, wave_full, wave_full)

    def send_out_one(field):
        return lax.all_to_all(field, "wide", split_axis=4, concat_axis=3, tiled=True)

    def send_home_one(field):
        return lax.all_to_all(field, "wide", split_axis=3, concat_axis=4, tiled=True)

    results = [maxwell_pass(spectrum, waves, inv_diag, inv_corr, send_out_one, send_home_one)]
    applied_st, space, weighted = [
        jnp.concatenate([entry[slot] for entry in results], axis=1) for slot in range(3)
    ]
    applied = jnp.stack([applied_st[0], applied_st[1]], axis=1).astype(jnp.bfloat16)
    scale_all = 1.0 / float(grid_len * grid_len * grid_len)
    left_re = space[0].reshape(band_count, -1)
    left_im = space[1].reshape(band_count, -1)
    right_re = weighted[0].reshape(band_count, -1)
    right_im = weighted[1].reshape(band_count, -1)
    part_re = jnp.einsum("an,bn->ab", left_re, right_re, precision=highest) + jnp.einsum(
        "an,bn->ab", left_im, right_im, precision=highest
    )
    part_im = jnp.einsum("an,bn->ab", left_re, right_im, precision=highest) - jnp.einsum(
        "an,bn->ab", left_im, right_re, precision=highest
    )
    total_re, total_im = lax.psum((part_re, part_im), "wide")
    rayleigh = jnp.stack([total_re * scale_all, total_im * scale_all], axis=0)
    return (applied, rayleigh)


def solution(mesh):
    in_specs = (
        P("groups", None, None, "wide", None, None),
        P("groups", None, None, "wide", None, None),
        P("groups", None, "wide", None),
        P("groups", None, "wide", None),
    )
    out_specs = (P("groups", None, None, "wide", None, None), P("groups", None, None))
    return jax.shard_map(
        per_device, mesh=mesh, in_specs=in_specs, out_specs=out_specs, check_vma=False
    )
```

profile of v0, /device:TPU:0, one launch (start us, length us, event | category | flops | bytes accessed | tf_op | source)
XLA Modules:
  0.0 763.4 jit_solution(15540134172055891031)
XLA Ops:
  0.6 10.4 %fusion.89 = (bf16[4,1,3,6,192,192]{5,4,3,2,1,0:T(8,128)(2,1)}, bf16[4,1,3,6,192,192]{5,4,3,2,1,0:T(8,128)(2,1)}) fusion(bf16[4,2,3,6,192,192]{5,4,3,2,1,0:T(8,128)(2,1)} %param.5), kind=kLoop, calls=%fused_computation.148 | loop fusion | bytes 21233664 | tf_op jit(solution)/shard_map/slice | solution.py:132
  11.0 13.4 %reshape.684 = bf16[2654208]{0:T(1024)(128)(2,1)} reshape(bf16[4,1,3,6,192,192]{5,4,3,2,1,0:T(8,128)(2,1)} %get-tuple-element.13) | data formatting | bytes 10616832
  24.4 21.1 %fusion.39 = f32[4,4]{0,1:T(4,128)S(1)} fusion(bf16[4,1,3,6,192,192]{5,4,3,2,1,0:T(8,128)(2,1)} %get-tuple-element.13), kind=kOutput, calls=%fused_computation.71 | convolution fusion | flops 21233664 | bytes 5308480 | tf_op jit(solution)/shard_map/an,bn->ab/dot_general | solution.py:80
  45.5 13.8 %fusion.41 = f32[4,4]{0,1:T(4,128)S(1)} fusion(bf16[4,1,3,6,192,192]{5,4,3,2,1,0:T(8,128)(2,1)S(1)} %bitcast.309, bf16[4,1,3,6,192,192]{5,4,3,2,1,0:T(8,128)(2,1)} %get-tuple-element.13), kind=kOutput, calls=%fused_computation.73 | convolution fusion | flops 21233664 | bytes 10616896 | tf_op jit(solution)/shard_map/an,bn->ab/dot_general | solution.py:80
  59.3 13.3 %reshape.688 = bf16[2654208]{0:T(1024)(128)(2,1)} reshape(bf16[4,1,3,6,192,192]{5,4,3,2,1,0:T(8,128)(2,1)} %get-tuple-element.12) | data formatting | bytes 10616832
  72.7 6.9 reshape_squeeze.16
  79.6 21.3 %fusion.43 = f32[4,4]{0,1:T(4,128)S(1)} fusion(f32[4,4]{0,1:T(4,128)S(1)} %fusion.39, bf16[4,1,3,6,192,192]{5,4,3,2,1,0:T(8,128)(2,1)} %get-tuple-element.12), kind=kOutput, calls=%fused_computation.75 | convolution fusion | flops 21233680 | bytes 5308544 | tf_op jit(solution)/shard_map/an,bn->ab/dot_general | solution.py:80
  101.0 14.4 %fusion.44 = f32[4,4]{0,1:T(4,128)S(1)} fusion(f32[4,4]{0,1:T(4,128)S(1)} %fusion.41, bf16[4,1,3,6,192,192]{5,4,3,2,1,0:T(8,128)(2,1)} %get-tuple-element.13, bf16[4,1,3,6,192,192]{5,4,3,2,1,0:T(8,128)(2,1)S(1)} %bitcast.311), kind=kOutput, calls=%fused_computation.76 | convolution fusion | flops 21233680 | bytes 10616960 | tf_op jit(solution)/shard_map/an,bn->ab/dot_general | solution.py:80
  119.0 6.8 reshape_squeeze.7
  127.9 7.8 %convolution_bitcast_fusion = f32[4]{0:T(128)S(1)} fusion(bf16[4,663552]{1,0:T(4,128)(2,1)} %reshape_squeeze.16, bf16[663552]{0:T(1024)(128)(2,1)} %reshape.686), kind=kOutput, calls=%fused_computation.77 | convolution fusion | flops 5308416 | bytes 6635536 | tf_op jit(solution)/shard_map/an,bn->ab/dot_general | solution.py:80
  135.8 7.4 convolution_bitcast_fusion.2
  143.2 5.9 fusion.48
  155.0 42.2 %all-reduce.1 = (f32[4,4]{0,1:T(4,128)S(1)}, f32[4,4]{0,1:T(4,128)S(1)}, f32[4,1]{0,1:T(1,128)S(1)}, f32[4,1]{0,1:T(1,128)S(1)}) all-reduce(f32[4,4]{0,1:T(4,128)S(1)} %fusion.43, f32[4,4]{0,1:T(4,128)S(1)} %fusion.44, f32[4,1]{0,1:T(1,128)S(1)} %fusion.48, f32[4,1]{0,1:T(1,128)S(1)} %fusion.46), channel_id=1, replica_groups=mesh['groups'=1,'wide'=32] {'wide'}, use_global_device_ids=true, to_apply=%region_0.0 | all-reduce | flops 40 | bytes 320 | tf_op jit(solution)/shard_map/psum | solution.py:138
  200.6 10.5 %fusion.82 = f32[1,663552]{1,0:T(1,128)S(1)} fusion(bf16[4,663552]{1,0:T(4,128)(2,1)} %reshape_squeeze.16, f32[8]{0:T(128)S(1)} %convolution_bitcast_fusion.4), kind=kOutput, calls=%fused_computation.141 | convolution fusion | flops 31850496 | bytes 7962656 | tf_op jit(solution)/shard_map/ab,an->bn/dot_general | solution.py:101
  211.1 10.5 %fusion.80 = f32[1,663552]{1,0:T(1,128)S(1)} fusion(bf16[4,663552]{1,0:T(4,128)(2,1)} %reshape_squeeze.7, f32[8]{0:T(128)S(1)} %convolution_bitcast_fusion.4), kind=kOutput, calls=%fused_computation.139 | convolution fusion | flops 31850496 | bytes 7962656 | tf_op jit(solution)/shard_map/ab,an->bn/dot_general | solution.py:100
  221.7 11.7 %fusion.83 = f32[1,663552]{1,0:T(1,128)} fusion(bf16[4,663552]{1,0:T(4,128)(2,1)} %reshape_squeeze.7, f32[8]{0:T(128)S(1)} %convolution_bitcast_fusion.4), kind=kOutput, calls=%fused_computation.142 | convolution fusion | flops 31850496 | bytes 7962656 | tf_op jit(solution)/shard_map/ab,an->bn/dot_general | solution.py:106
  233.4 9.7 %fusion.81 = f32[1,663552]{1,0:T(1,128)} fusion(bf16[4,663552]{1,0:T(4,128)(2,1)S(1)} %bitcast.315, f32[8]{0:T(128)S(1)} %convolution_bitcast_fusion.4), kind=kOutput, calls=%fused_computation.140 | convolution fusion | flops 31850496 | bytes 7962656 | tf_op jit(solution)/shard_map/ab,an->bn/dot_general | solution.py:105
  267.5 12.0 %fusion = f32[2,192,3,6,192,1]{4,1,5,3,2,0:T(8,128)S(1)} fusion(f32[1,1,3,6,192,192]{5,4,0,3,2,1:T(8,128)S(1)} %maximum_bitcast_fusion.2, f32[1,1,3,6,192,192]{5,4,0,3,2,1:T(8,128)S(1)} %fusion.21, f32[1,2,192,192]{2,3,0,1:T(8,128)S(1)} %get-tuple-element.42, f32[1,2,192,192]{2,3,0,1:T(8,128)S(1)} %get-tuple-element.43), kind=kOutput, calls=%fused_computation.1 | convolution fusion | flops 6116769792 | bytes 11206656 | tf_op jit(solution)/shard_map/pbcxyk,pqkn->qbcxyn/dot_general | solution.py:76
  279.6 13.5 %fusion.23 = f32[2,1,3,6,192,192]{5,4,3,2,0,1:T(8,128)} fusion(f32[2,192,3,6,192,1]{4,1,5,3,2,0:T(8,128)S(1)} %fusion, f32[1,2,192,192]{2,3,0,1:T(8,128)S(1)} %get-tuple-element.42, f32[1,2,192,192]{2,3,0,1:T(8,128)S(1)} %get-tuple-element.43), kind=kOutput, calls=%fused_computation.41 | convolution fusion | flops 6115442688 | bytes 11206656 | tf_op jit(solution)/shard_map/pbcxkz,pqkn->qbcxnz/dot_general | solution.py:75
  293.1 11.4 %copy.97 = f32[2,1,3,6,192,192]{5,0,3,2,1,4:T(2,128)} copy(f32[2,1,3,6,192,192]{5,4,3,2,0,1:T(8,128)} %fusion.23) | data formatting | bytes 10616832 | tf_op jit(solution)/shard_map/pbcxkz,pqkn->qbcxnz/transpose | solution.py:75
  315.1 151.6 %all-to-all-done = f32[2,1,3,6,192,192]{5,0,3,2,1,4:T(2,128)} async-done(((f32[2,1,3,6,192,192]{5,0,3,2,1,4:T(2,128)}), f32[2,1,3,6,192,192]{5,0,3,2,1,4:T(2,128)}, u32[]{:S(2)}, u32[]{:S(2)}) %all-to-all-start) | async-done | bytes 5308448 | tf_op jit(solution)/shard_map/all_to_all | solution.py:149
  466.7 9.8 %copy.98 = f32[2,1,3,6,192,192]{5,0,4,3,2,1:T(2,128)} copy(f32[2,1,3,6,192,192]{5,0,3,2,1,4:T(2,128)} %all-to-all-done) | data formatting | bytes 10616832 | tf_op jit(solution)/shard_map/all_to_all | solution.py:149
  476.5 8.6 %copy.99 = f32[2,1,3,32,6,6,192]{6,0,5,4,3,2,1:T(2,128)} copy(f32[2,1,3,32,6,6,192]{6,0,5,3,4,2,1:T(2,128)} %bitcast.312) | data formatting | bytes 10616832 | tf_op jit(solution)/shard_map/all_to_all | solution.py:149
  485.1 14.5 %fusion.26 = f32[2,1,3,192,6,192]{5,3,4,2,0,1:T(8,128)S(1)} fusion(f32[2,3,192,6,192]{4,0,3,2,1:T(2,128)} %bitcast.306, f32[1,2,192,192]{2,3,0,1:T(8,128)S(1)} %copy-done.3, f32[1,2,192,192]{2,3,0,1:T(8,128)S(1)} %copy-done.5), kind=kOutput, calls=%fused_computation.42 | convolution fusion | flops 6115442688 | bytes 11206656 | tf_op jit(solution)/shard_map/pbckyz,pqkn->qbcnyz/dot_general | solution.py:73
  505.9 13.5 %fusion.29 = f32[2,1,3,192,6,192]{5,3,4,2,0,1:T(8,128)} fusion(f32[2,3,192,6,192]{4,2,3,1,0:T(8,128)S(1)} %get-tuple-element.18, f32[1,2,192,192]{2,3,1,0:T(8,128)S(1)} %copy-done.7, f32[1,2,192,192]{2,3,1,0:T(8,128)S(1)} %copy-done.6), kind=kOutput, calls=%fused_computation.43 | convolution fusion | flops 6115442688 | bytes 11206656 | tf_op jit(solution)/shard_map/pbckyz,pqkn->qbcnyz/dot_general | solution.py:73
  519.4 11.3 %copy.103 = f32[2,1,3,192,6,192]{5,0,4,2,1,3:T(2,128)} copy(f32[2,1,3,192,6,192]{5,3,4,2,0,1:T(8,128)} %fusion.29) | data formatting | bytes 10616832 | tf_op jit(solution)/shard_map/pbckyz,pqkn->qbcnyz/transpose | solution.py:73
  534.5 6.4 multiply_reduce_fusion.2
  543.6 167.6 %all-reduce = (f32[1,1]{1,0:T(1,128)}, f32[1,1]{1,0:T(1,128)}) all-reduce(f32[1,1]{1,0:T(1,128)} %bitcast.102, f32[1,1]{1,0:T(1,128)} %bitcast.99), channel_id=1, replica_groups=mesh['groups'=1,'wide'=32] {'wide'}, use_global_device_ids=true, to_apply=%region_7.8 | all-reduce | flops 2 | bytes 16 | tf_op jit(solution)/shard_map/psum | solution.py:170
  713.0 8.3 %copy.104 = f32[2,1,3,192,6,192]{5,0,4,3,2,1:T(2,128)} copy(f32[2,1,3,192,6,192]{5,0,4,2,1,3:T(2,128)} %all-to-all-done.1) | data formatting | bytes 10616832 | tf_op jit(solution)/shard_map/all_to_all | solution.py:152
  721.3 9.4 %copy.105 = f32[2,1,3,6,32,6,192]{6,0,5,4,3,2,1:T(2,128)} copy(f32[2,1,3,6,32,6,192]{6,0,5,3,4,2,1:T(2,128)} %bitcast.313) | data formatting | bytes 10616832 | tf_op jit(solution)/shard_map/all_to_all | solution.py:152
  730.7 14.7 %fusion.32 = f32[2,3,6,192,192]{4,3,2,1,0:T(8,128)S(1)} fusion(f32[2,3,6,192,192]{4,0,3,2,1:T(2,128)} %bitcast.307, f32[1,2,192,192]{2,3,1,0:T(8,128)S(1)} %copy-done.7, f32[1,2,192,192]{2,3,1,0:T(8,128)S(1)} %copy-done.6), kind=kOutput, calls=%fused_computation.44 | convolution fusion | flops 6115442688 | bytes 11206656 | tf_op jit(solution)/shard_map/pbcxkz,pqkn->qbcxnz/dot_general | solution.py:75
  745.4 12.4 %fusion.35 = f32[2,1,3,6,192,192]{5,4,3,2,1,0:T(8,128)S(1)} fusion(f32[2,3,6,192,192]{4,3,2,1,0:T(8,128)S(1)} %fusion.32, f32[1,2,192,192]{2,3,1,0:T(8,128)S(1)} %copy-done.7, f32[1,2,192,192]{2,3,1,0:T(8,128)S(1)} %copy-done.6), kind=kOutput, calls=%fused_computation.45 | convolution fusion | flops 6115442688 | bytes 11206656 | tf_op jit(solution)/shard_map/pbcxyk,pqkn->qbcxyn/dot_general | solution.py:76
  (107 shorter events, 66.1 us)
Async XLA Ops:
  11.0 34.5 %slice-start = ((s8[7077888]{0:T(1024)(128)(4,1)}), s8[2883584]{0:T(1024)(128)(4,1)S(1)}, s32[]{:S(2)}) async-start(s8[7077888]{0:T(1024)(128)(4,1)} %bitcast.308), calls=%async_computation.2 | async-start | bytes 5767168
  24.4 21.1 %slice-start.1 = ((s8[7077888]{0:T(1024)(128)(4,1)}), s8[4194304]{0:T(1024)(128)(4,1)S(1)}, s32[]{:S(2)}) async-start(s8[7077888]{0:T(1024)(128)(4,1)} %bitcast.308), calls=%async_computation.3 | async-start | bytes 8388608
  72.7 28.3 %slice-start.2 = ((s8[7077888]{0:T(1024)(128)(4,1)}), s8[2883584]{0:T(1024)(128)(4,1)S(1)}, s32[]{:S(2)}) async-start(s8[7077888]{0:T(1024)(128)(4,1)} %bitcast.310), calls=%async_computation.4 | async-start | bytes 5767168
  79.6 21.4 %slice-start.3 = ((s8[7077888]{0:T(1024)(128)(4,1)}), s8[4194304]{0:T(1024)(128)(4,1)S(1)}, s32[]{:S(2)}) async-start(s8[7077888]{0:T(1024)(128)(4,1)} %bitcast.310), calls=%async_computation.5 | async-start | bytes 8388608
  101.0 14.4 %copy-start.16 = (bf16[1,2,3,6,192,192]{5,4,3,2,1,0:T(8,128)(2,1)S(1)}, bf16[1,2,3,6,192,192]{5,4,3,2,1,0:T(8,128)(2,1)}, u32[]{:S(2)}) copy-start(bf16[1,2,3,6,192,192]{5,4,3,2,1,0:T(8,128)(2,1)} %param.4) | copy-start | bytes 7962628
  127.9 15.2 %copy-start.8 = (bf16[663552]{0:T(1024)(128)(2,1)}, bf16[663552]{0:T(1024)(128)(2,1)S(1)}, u32[]{:S(2)}) copy-start(bf16[663552]{0:T(1024)(128)(2,1)S(1)} %reshape.690) | copy-start | bytes 3981316
  127.9 15.2 %slice-start.6 = ((s8[5308416]{0:T(1024)(128)(4,1)}), s8[4194304]{0:T(1024)(128)(4,1)S(1)}, s32[]{:S(2)}) async-start(s8[5308416]{0:T(1024)(128)(4,1)} %bitcast.316), calls=%async_computation.8 | async-start | bytes 8388608
  135.8 7.4 slice-start.7
  143.1 6.0 copy-start.9
  211.1 22.3 %slice-start.4 = ((s8[5308416]{0:T(1024)(128)(4,1)}), s8[4194304]{0:T(1024)(128)(4,1)S(1)}, s32[]{:S(2)}) async-start(s8[5308416]{0:T(1024)(128)(4,1)} %bitcast.314), calls=%async_computation.6 | async-start | bytes 8388608
  221.6 11.7 %slice-start.5 = ((s8[5308416]{0:T(1024)(128)(4,1)}), s8[1114112]{0:T(1024)(128)(4,1)S(1)}, s32[]{:S(2)}) async-start(s8[5308416]{0:T(1024)(128)(4,1)} %bitcast.314), calls=%async_computation.7 | async-start | bytes 2228224
  265.3 1.0 copy-start.19
  265.3 1.1 copy-start.20
  265.3 1.2 copy-start.21
  265.3 1.2 copy-start.22
  267.5 12.0 %copy-start.2 = (f32[1,2,192,192]{2,3,0,1:T(8,128)}, f32[1,2,192,192]{2,3,0,1:T(8,128)S(1)}, u32[]{:S(2)}) copy-start(f32[1,2,192,192]{2,3,0,1:T(8,128)S(1)} %get-tuple-element.42) | copy-start | bytes 884740
  267.5 12.0 %copy-start.4 = (f32[1,2,192,192]{2,3,0,1:T(8,128)}, f32[1,2,192,192]{2,3,0,1:T(8,128)S(1)}, u32[]{:S(2)}) copy-start(f32[1,2,192,192]{2,3,0,1:T(8,128)S(1)} %get-tuple-element.43) | copy-start | bytes 884740
  304.5 4.9 copy-start.1
  304.5 162.3 %all-to-all-start = ((f32[2,1,3,6,192,192]{5,0,3,2,1,4:T(2,128)}), f32[2,1,3,6,192,192]{5,0,3,2,1,4:T(2,128)}, u32[]{:S(2)}, u32[]{:S(2)}) async-start(f32[2,1,3,6,192,192]{5,0,3,2,1,4:T(2,128)} %copy.97), calls=%async_computation | async-start | bytes 14155776 | tf_op jit(solution)/shard_map/all_to_all | solution.py:149
  309.4 3.3 copy-start.17
  476.5 8.6 %copy-start.3 = (f32[1,2,192,192]{2,3,0,1:T(8,128)S(1)}, f32[1,2,192,192]{2,3,0,1:T(8,128)}, u32[]{:S(2)}) copy-start(f32[1,2,192,192]{2,3,0,1:T(8,128)} %copy-done.2) | copy-start | bytes 884740
  476.5 8.6 %copy-start.5 = (f32[1,2,192,192]{2,3,0,1:T(8,128)S(1)}, f32[1,2,192,192]{2,3,0,1:T(8,128)}, u32[]{:S(2)}) copy-start(f32[1,2,192,192]{2,3,0,1:T(8,128)} %copy-done.4) | copy-start | bytes 884740
  485.1 14.5 %copy-start.10 = (f32[192,6,192]{2,0,1:T(8,128)S(1)}, f32[192,6,192]{2,0,1:T(8,128)}, u32[]{:S(2)}) copy-start(f32[192,6,192]{2,0,1:T(8,128)} %get-tuple-element.36) | copy-start | bytes 2654212
  485.1 14.5 %copy-start.11 = (f32[192,6,192]{2,0,1:T(8,128)S(1)}, f32[192,6,192]{2,0,1:T(8,128)}, u32[]{:S(2)}) copy-start(f32[192,6,192]{2,0,1:T(8,128)} %get-tuple-element.37) | copy-start | bytes 2654212
  485.1 14.5 %copy-start.12 = (f32[192,6,192]{2,0,1:T(8,128)S(1)}, f32[192,6,192]{2,0,1:T(8,128)}, u32[]{:S(2)}) copy-start(f32[192,6,192]{2,0,1:T(8,128)} %get-tuple-element.38) | copy-start | bytes 2654212
  485.1 14.5 %copy-start.13 = (f32[192,6,192]{2,0,1:T(8,128)S(1)}, f32[192,6,192]{2,0,1:T(8,128)}, u32[]{:S(2)}) copy-start(f32[192,6,192]{2,0,1:T(8,128)} %get-tuple-element.21) | copy-start | bytes 2654212
  485.1 14.5 %copy-start.14 = (f32[192,6,192]{2,0,1:T(8,128)S(1)}, f32[192,6,192]{2,0,1:T(8,128)}, u32[]{:S(2)}) copy-start(f32[192,6,192]{2,0,1:T(8,128)} %get-tuple-element.22) | copy-start | bytes 2654212
  485.1 14.5 %copy-start.15 = (f32[192,6,192]{2,0,1:T(8,128)S(1)}, f32[192,6,192]{2,0,1:T(8,128)}, u32[]{:S(2)}) copy-start(f32[192,6,192]{2,0,1:T(8,128)} %get-tuple-element.23) | copy-start | bytes 2654212
  499.6 2.9 copy-start
  502.5 3.4 copy-start.6
  502.5 3.4 copy-start.7
  530.7 182.4 %all-to-all-start.1 = ((f32[2,1,3,192,6,192]{5,0,4,2,1,3:T(2,128)}), f32[2,1,3,192,6,192]{5,0,4,2,1,3:T(2,128)}, u32[]{:S(2)}, u32[]{:S(2)}) async-start(f32[2,1,3,192,6,192]{5,0,4,2,1,3:T(2,128)} %copy.103), calls=%async_computation.1 | async-start | bytes 14155776 | tf_op jit(solution)/shard_map/all_to_all | solution.py:152
  (1 other events, 0.9 us)
where the time goes:
time: 773 us; the launch traced here: 763 us
  matrix products  221 us (29%)
  blocking collectives  210 us (27%)
  waiting for transfers between devices  152 us (20%)
  local copies, waits for them, and re-layouts  130 us (17%)
  other arithmetic  37.5 us (5%)
  starting transfers between devices  8.77 us (1%)
    psum x1, blocking collectives, per_device(): total_re, total_im = lax.psum((part_re, part_im), 'wide')  168 us
    all_to_all x1, waiting for transfers between devices, send_out_one(): lax.all_to_all(field, 'wide', split_axis=4, concat_axis=3, tiled=True)  152 us
    dot_general x8, matrix products, inner_sum(): jnp.einsum('an,bn->ab', left_rows, right_rows, preferred_element_type=jnp...  97.7 us
    psum x1, blocking collectives, per_device(): gram_sums = lax.psum((gram_a, gram_q, proj_re, proj_im), 'wide')  42.2 us
    unnamed x66, local copies, waits for them, and re-layouts  35.7 us
    dot_general x2, matrix products, transform(): return jnp.einsum('pbcxkz,pqkn->qbcxnz', stacked, table, precision=highest)  28.2 us
    dot_general x2, matrix products, transform(): return jnp.einsum('pbckyz,pqkn->qbcnyz', stacked, table, precision=highest)  28 us
    dot_general x2, matrix products, transform(): return jnp.einsum('pbcxyk,pqkn->qbcxyn', stacked, table, precision=highest)  24.4 us
  transfers between devices with their start and end apart: 2, of which 1 were waited for; matrix products, arithmetic and copies ran while one was open for 1% of the time, Pallas kernels for 0%

commit v1 on v0

v1 whole, which is shorter than its diff:
```python
import functools
import math

import jax
import jax.numpy as jnp
import numpy as np
from jax import lax
from jax.experimental import pallas as pl
from jax.experimental.pallas import tpu as pltpu
from jax.sharding import PartitionSpec as P

HI = lax.Precision.HIGHEST
F32 = jnp.float32
BF16 = jnp.bfloat16
VMEM_LIMIT = 56 * 1024 * 1024


def signed(length):
    g = np.arange(length)
    return np.where(g < length // 2, g, g - length).astype(np.float32) / np.float32(length / 2.0)


def cos_sin(length, orient):
    g = np.arange(length)
    ang = (g[:, None] * g[None, :] % length) * (2.0 * math.pi / length)
    return np.cos(ang) / math.sqrt(length), orient * np.sin(ang) / math.sqrt(length)


def split_np(table):
    table = table.astype(np.float32)
    high = table.astype(BF16)
    low = (table - high.astype(np.float32)).astype(BF16)
    return np.stack([high, low])


def lane_order(length):
    cut = 2 * length // 3
    part = np.concatenate([np.zeros(length), np.ones(length)]).astype(int)
    pos = np.concatenate([np.arange(length), np.arange(cut, length), np.arange(cut)])
    return part, pos


def right_table(length, orient):
    cos, sin = cos_sin(length, orient)
    full = np.block([[cos, sin], [-sin, cos]])
    part, pos = lane_order(length)
    return full[:, part * length + pos]


def right_table_back(length, orient):
    cos, sin = cos_sin(length, orient)
    full = np.block([[cos, sin], [-sin, cos]])
    part, pos = lane_order(length)
    return full[part * length + pos, :]


def left_table(length, orient, perm_rows=None, perm_cols=None):
    cos, sin = cos_sin(length, orient)
    if perm_rows is not None:
        cos, sin = cos[perm_rows], sin[perm_rows]
    if perm_cols is not None:
        cos, sin = cos[:, perm_cols], sin[:, perm_cols]
    return np.concatenate([cos, sin], axis=1)


def split(x):
    high = x.astype(BF16)
    low = (x - high.astype(F32)).astype(BF16)
    return high, low


def dot(a, b):
    return jnp.dot(a, b, preferred_element_type=F32)


def dot3(a, b):
    return dot(a[0], b[0]) + (dot(a[0], b[1]) + dot(a[1], b[0]))


def times_i(tiles):
    t0, t1, t2 = tiles
    half = t1.shape[1] // 2
    lane = lax.broadcasted_iota(jnp.int32, t1.shape, 1)
    mid = pltpu.roll(t1, half, 1)
    mid = jnp.where(lane < half, -mid, mid)
    return [-t2, mid, t0]


def left_dft(table, tiles, turned):
    rows = jnp.concatenate(
        [jnp.concatenate(tiles, axis=1), jnp.concatenate(turned, axis=1)], axis=0
    )
    return dot3(table, split(rows))


def gram_kernel(kept, locked_ref, trial_ref, out_ref, acc_ref):
    step = pl.program_id(0)
    grid_len = locked_ref.shape[4]
    fields = 2 * kept + 2

    @pl.when(step == 0)
    def _():
        acc_ref[...] = jnp.zeros_like(acc_ref)

    total = None
    for comp in range(3):
        for at in range(0, grid_len, 16):
            parts = [locked_ref[k, p, comp, 0, at:at + 16, :] for p in range(2) for k in range(kept)]
            parts += [trial_ref[0, p, comp, 0, at:at + 16, :] for p in range(2)]
            rows = jnp.concatenate(parts, axis=0)
            one = lax.dot_general(
                rows, rows, (((1,), (1,)), ((), ())), preferred_element_type=F32
            )
            total = one if total is None else total + one
    acc_ref[...] += total

    @pl.when(step == pl.num_programs(0) - 1)
    def _():
        acc = acc_ref[...]
        size = fields * 16
        row = lax.broadcasted_iota(jnp.int32, (size, size), 0)
        col = lax.broadcasted_iota(jnp.int32, (size, size), 1)
        kept_only = jnp.where((row & 15) == (col & 15), acc, 0.0)
        by_row = jnp.sum(kept_only.reshape(fields, 16, size), axis=1)
        pick_r = lax.broadcasted_iota(jnp.int32, (size, 128), 0)
        pick_c = lax.broadcasted_iota(jnp.int32, (size, 128), 1)
        pick = jnp.where((pick_r >> 4) == pick_c, 1.0, 0.0)
        small = jnp.dot(by_row, pick, precision=HI, preferred_element_type=F32)
        out_ref[...] = jnp.concatenate([small, jnp.zeros((16 - fields, 128), F32)], axis=0)


def peer_of(me, k, n):
    if n & (n - 1) == 0:
        return lax.bitwise_xor(me, k)
    return lax.rem(me + k, n)


def greet(me, n):
    barrier = pltpu.get_barrier_semaphore()

    def hello(k, carry):
        pl.semaphore_signal(
            barrier,
            inc=1,
            device_id={"wide": lax.rem(me + k, n)},
            device_id_type=pl.DeviceIdType.MESH,
        )
        return carry

    lax.fori_loop(1, n, hello, 0)
    pl.semaphore_wait(barrier, n - 1)


def sum_kernel(n, x_ref, o_ref, buf_ref, send, recv):
    me = lax.axis_index("wide")
    buf_ref[0] = x_ref[...]
    greet(me, n)

    def make(k):
        peer = lax.rem(me + k, n)
        return pltpu.make_async_remote_copy(
            src_ref=x_ref,
            dst_ref=buf_ref.at[k],
            send_sem=send.at[k],
            recv_sem=recv.at[k],
            device_id={"wide": peer},
            device_id_type=pl.DeviceIdType.MESH,
        )

    def go(k, carry):
        make(k).start()
        return carry

    def finish(k, carry):
        make(k).wait()
        return carry

    lax.fori_loop(1, n, go, 0)
    lax.fori_loop(1, n, finish, 0)
    o_ref[...] = jnp.sum(buf_ref[...], axis=0)


def sum_small(x, n):
    return pl.pallas_call(
        functools.partial(sum_kernel, n),
        out_shape=jax.ShapeDtypeStruct(x.shape, x.dtype),
        in_specs=[pl.BlockSpec(memory_space=pltpu.VMEM)],
        out_specs=pl.BlockSpec(memory_space=pltpu.VMEM),
        scratch_shapes=[
            pltpu.VMEM((n,) + x.shape, x.dtype),
            pltpu.SemaphoreType.DMA((n,)),
            pltpu.SemaphoreType.DMA((n,)),
        ],
        compiler_params=pltpu.CompilerParams(collective_id=0, has_side_effects=True),
    )(x)


def out_kernel(sizes, coef_ref, wave_ref, locked_ref, trial_ref, qy_ref, qz_ref, tz_ref, ty_ref, out_ref):
    n, rows, lx, ly, kept, grid_len = sizes
    step = pl.program_id(0)
    qx = wave_ref[step]
    qy = qy_ref[...]
    qz = qz_ref[...]
    one = [coef_ref[k] for k in range(kept)]
    two = [coef_ref[kept + k] for k in range(kept)]
    real, imag = [], []
    for comp in range(3):
        re = trial_ref[0, 0, comp, 0].astype(F32)
        im = trial_ref[0, 1, comp, 0].astype(F32)
        for k in range(kept):
            lre = locked_ref[k, 0, comp, 0].astype(F32)
            lim = locked_ref[k, 1, comp, 0].astype(F32)
            re = re - one[k] * lre + two[k] * lim
            im = im - one[k] * lim - two[k] * lre
        real.append(re)
        imag.append(im)

    def cross(v):
        return [qy * v[2] - qz * v[1], qz * v[0] - qx * v[2], qx * v[1] - qy * v[0]]

    curl_re = [-v for v in cross(imag)]
    curl_im = cross(real)
    for comp in range(3):
        out = dot3(split(curl_re[comp]), (tz_ref[0, :grid_len], tz_ref[1, :grid_len]))
        out += dot3(split(curl_im[comp]), (tz_ref[0, grid_len:], tz_ref[1, grid_len:]))
        tiles = [out[:, t * 128:(t + 1) * 128] for t in range(3)]
        out = left_dft((ty_ref[0], ty_ref[1]), tiles, times_i(tiles))
        for j in range(ly):
            for t in range(3):
                at = t * rows + step * (3 * ly) + comp * ly + j
                out_ref[pl.ds(at, n, stride=3 * rows), :] = out[j * n:(j + 1) * n, t * 128:(t + 1) * 128]


def mid_kernel(sizes, x_ref, diag_ref, corr_ref, ti_ref, tf_ref, out_ref, acc_ref):
    n, rows, lx, ly, kept, grid_len = sizes
    step = pl.program_id(0)

    @pl.when(step == 0)
    def _():
        acc_ref[...] = jnp.zeros_like(acc_ref)

    space = []
    for comp in range(3):
        tiles = []
        for t in range(3):
            at = [t * rows + x * (3 * ly) + comp * ly + step for x in range(lx)]
            tiles.append(
                jnp.concatenate([x_ref[pl.ds(a, n, stride=3 * rows), :] for a in at], axis=0)
            )
        out = left_dft((ti_ref[0], ti_ref[1]), tiles, times_i(tiles))
        space.append([out[:, t * 128:(t + 1) * 128] for t in range(3)])

    def lanes(e):
        tail = e[:, 128:]
        return [e[:, :128], jnp.concatenate([tail, tail], axis=1)]

    dx, dy, dz = diag_ref[0, 0], diag_ref[1, 0], diag_ref[2, 0]
    exy = lanes(corr_ref[0, 0] * jnp.sqrt(dx * dy))
    exz = lanes(corr_ref[1, 0] * jnp.sqrt(dx * dz))
    eyz = lanes(corr_ref[2, 0] * jnp.sqrt(dy * dz))
    exx, eyy, ezz = lanes(dx), lanes(dy), lanes(dz)
    matrix = [[exx, exy, exz], [exy, eyy, eyz], [exz, eyz, ezz]]
    sum_re = jnp.zeros((grid_len, 128), F32)
    sum_im = jnp.zeros((grid_len, 128), F32)
    for comp in range(3):
        tiles = []
        for t in range(3):
            e = [matrix[comp][b][t % 2] for b in range(3)]
            tiles.append(e[0] * space[0][t] + e[1] * space[1][t] + e[2] * space[2][t])
        turned = times_i(tiles)
        for t in range(3):
            sum_re += space[comp][t] * tiles[t]
            sum_im -= space[comp][t] * turned[t]
        out = left_dft((tf_ref[0], tf_ref[1]), tiles, turned)
        for x in range(lx):
            for t in range(3):
                at = t * rows + x * (3 * ly) + comp * ly + step
                out_ref[pl.ds(at, n, stride=3 * rows), :] = out[x * n:(x + 1) * n, t * 128:(t + 1) * 128]
    acc_ref[0:1] += jnp.sum(sum_re, axis=0, keepdims=True)
    acc_ref[1:2] += jnp.sum(sum_im, axis=0, keepdims=True)

    @pl.when(step == pl.num_programs(0) - 1)
    def _():
        for t in range(3):
            for r in range(3 * lx * ly, rows):
                value = jnp.broadcast_to(acc_ref[min(t, 1):min(t, 1) + 1], (n, 128))
                out_ref[pl.ds(t * rows + r, n, stride=3 * rows), :] = value


def home_kernel(sizes, wave_ref, x_ref, qy_ref, qz_ref, ty_ref, tz_ref, out_ref, ray_ref):
    n, rows, lx, ly, kept, grid_len = sizes
    step = pl.program_id(0)
    qx = wave_ref[step]
    qy = qy_ref[...]
    qz = qz_ref[...]
    real, imag = [], []
    for comp in range(3):
        tiles = []
        for t in range(3):
            at = [t * rows + step * (3 * ly) + comp * ly + j for j in range(ly)]
            tiles.append(
                jnp.concatenate([x_ref[pl.ds(a, n, stride=3 * rows), :] for a in at], axis=0)
            )
        out = split(left_dft((ty_ref[0], ty_ref[1]), tiles, times_i(tiles)))
        real.append(dot3(out, (tz_ref[0], tz_ref[1])))
        imag.append(dot3(out, (tz_ref[2], tz_ref[3])))

    def cross(v):
        return [qy * v[2] - qz * v[1], qz * v[0] - qx * v[2], qx * v[1] - qy * v[0]]

    for comp, (a, b) in enumerate(zip(cross(imag), cross(real))):
        out_ref[0, 0, comp, 0] = (-a).astype(BF16)
        out_ref[0, 1, comp, 0] = b.astype(BF16)

    @pl.when(step == pl.num_programs(0) - 1)
    def _():
        for p in range(2):
            ray_ref[p * n:(p + 1) * n, :] = x_ref[pl.ds(p * rows + 3 * lx * ly, n, stride=3 * rows), :]


def swap_kernel(n, x_ref, o_ref, send, recv, here):
    me = lax.axis_index("wide")
    greet(me, n)

    def make(k):
        peer = peer_of(me, k, n)
        return pltpu.make_async_remote_copy(
            src_ref=x_ref.at[peer],
            dst_ref=o_ref.at[me],
            send_sem=send.at[k],
            recv_sem=recv.at[k],
            device_id={"wide": peer},
            device_id_type=pl.DeviceIdType.MESH,
        )

    def go(k, carry):
        make(k).start()
        return carry

    def finish(k, carry):
        make(k).wait()
        return carry

    lax.fori_loop(1, n, go, 0)
    own = pltpu.make_async_copy(x_ref.at[me], o_ref.at[me], here)
    own.start()
    own.wait()
    lax.fori_loop(1, n, finish, 0)


def exchange(flat, n):
    box = flat.reshape(n, flat.shape[0] // n, flat.shape[1])
    return lax.all_to_all(box, "wide", 0, 0, tiled=True).reshape(flat.shape)


def per_device(trial_bands, locked_bands, inv_diag, inv_corr):
    kept = locked_bands.shape[0]
    lx = trial_bands.shape[3]
    grid_len = trial_bands.shape[4]
    n = grid_len // lx
    ly = inv_diag.shape[2]
    rows = (3 * lx * ly + 8) // 8 * 8
    sizes = (n, rows, lx, ly, kept, grid_len)
    me = lax.axis_index("wide")
    fields = 2 * kept + 2

    def params():
        return pltpu.CompilerParams(vmem_limit_bytes=VMEM_LIMIT, dimension_semantics=("arbitrary",))

    def full(a):
        return pl.BlockSpec(a.shape, lambda i: (0,) * a.ndim)

    plane = lambda lead: pl.BlockSpec(
        (lead, 2, 3, 1, grid_len, grid_len), lambda i: (0, 0, 0, i, 0, 0)
    )
    smem = pl.BlockSpec(memory_space=pltpu.SMEM)

    part = pl.pallas_call(
        functools.partial(gram_kernel, kept),
        grid=(lx,),
        out_shape=jax.ShapeDtypeStruct((16, 128), F32),
        in_specs=[plane(kept), plane(1)],
        out_specs=pl.BlockSpec((16, 128), lambda i: (0, 0)),
        scratch_shapes=[pltpu.VMEM((fields * 16, fields * 16), F32)],
        compiler_params=params(),
    )(locked_bands, trial_bands)
    sums = sum_small(part, n)
    k2 = 2 * kept
    rr, ri = sums[:kept, :kept], sums[:kept, kept:k2]
    ir, ii = sums[kept:k2, :kept], sums[kept:k2, kept:k2]
    gram_a, gram_q = rr + ii, ir - ri
    proj_re = sums[:kept, k2:k2 + 1] + sums[kept:k2, k2 + 1:k2 + 2]
    proj_im = sums[:kept, k2 + 1:k2 + 2] - sums[kept:k2, k2:k2 + 1]
    gram = jnp.concatenate(
        [jnp.concatenate([gram_a, gram_q], axis=1), jnp.concatenate([gram_q.T, gram_a], axis=1)],
        axis=0,
    )
    rhs = jnp.concatenate([proj_re, proj_im], axis=0)
    lower = jnp.linalg.cholesky(gram)
    middle = lax.linalg.triangular_solve(lower, rhs, left_side=True, lower=True)
    coef = lax.linalg.triangular_solve(lower, middle, left_side=True, lower=True, transpose_a=True)
    coef = coef[:, 0]

    waves = signed(grid_len)
    wave_x = lax.dynamic_slice(jnp.asarray(waves), (me * lx,), (lx,))
    qy = jnp.asarray(np.broadcast_to(waves[:, None], (grid_len, grid_len)))
    qz = jnp.asarray(np.broadcast_to(waves[None, :], (grid_len, grid_len)))
    order_y = np.arange(grid_len).reshape(n, ly).T.reshape(-1)
    order_x = np.arange(grid_len).reshape(n, lx).T.reshape(-1)
    tz_out = jnp.asarray(split_np(right_table(grid_len, 1.0)))
    ty_out = jnp.asarray(split_np(left_table(grid_len, 1.0, perm_rows=order_y)))
    tx_in = jnp.asarray(split_np(left_table(grid_len, 1.0, perm_cols=order_x)))
    tx_out = jnp.asarray(split_np(left_table(grid_len, -1.0, perm_rows=order_x)))
    ty_in = jnp.asarray(split_np(left_table(grid_len, -1.0, perm_cols=order_y)))
    back = right_table_back(grid_len, -1.0)
    tz_in = jnp.asarray(
        np.concatenate([split_np(back[:, :grid_len]), split_np(back[:, grid_len:])])
    )

    flat_shape = jax.ShapeDtypeStruct((n * 3 * rows, 128), F32)
    flat_spec = pl.BlockSpec((n * 3 * rows, 128), lambda i: (0, 0))
    moved = pl.pallas_call(
        functools.partial(out_kernel, sizes),
        grid=(lx,),
        out_shape=flat_shape,
        in_specs=[smem, smem, plane(kept), plane(1), full(qy), full(qz), full(tz_out), full(ty_out)],
        out_specs=flat_spec,
        compiler_params=params(),
    )(coef, wave_x, locked_bands, trial_bands, qy, qz, tz_out, ty_out)
    moved = exchange(moved, n)

    slab = pl.BlockSpec((3, 1, grid_len, grid_len), lambda i: (0, i, 0, 0))
    weighted = pl.pallas_call(
        functools.partial(mid_kernel, sizes),
        grid=(ly,),
        out_shape=flat_shape,
        in_specs=[flat_spec, slab, slab, full(tx_in), full(tx_out)],
        out_specs=flat_spec,
        scratch_shapes=[pltpu.VMEM((8, 128), F32)],
        compiler_params=params(),
    )(moved, inv_diag.transpose(0, 2, 1, 3), inv_corr.transpose(0, 2, 1, 3), tx_in, tx_out)
    home = exchange(weighted, n)

    applied, ray = pl.pallas_call(
        functools.partial(home_kernel, sizes),
        grid=(lx,),
        out_shape=(
            jax.ShapeDtypeStruct(trial_bands.shape, BF16),
            jax.ShapeDtypeStruct((2 * n, 128), F32),
        ),
        in_specs=[smem, flat_spec, full(qy), full(qz), full(ty_in), full(tz_in)],
        out_specs=(plane(1), pl.BlockSpec((2 * n, 128), lambda i: (0, 0))),
        compiler_params=params(),
    )(wave_x, home, qy, qz, ty_in, tz_in)
    scale_all = 1.0 / float(grid_len * grid_len * grid_len)
    rayleigh = jnp.sum(ray.reshape(2, n * 128), axis=1).reshape(2, 1, 1) * scale_all
    return (applied, rayleigh)


def solution(mesh):
    in_specs = (
        P("groups", None, None, "wide", None, None),
        P("groups", None, None, "wide", None, None),
        P("groups", None, "wide", None),
        P("groups", None, "wide", None),
    )
    out_specs = (P("groups", None, None, "wide", None, None), P("groups", None, None))
    return jax.shard_map(
        per_device, mesh=mesh, in_specs=in_specs, out_specs=out_specs, check_vma=False
    )
```

time: 773 us -> 362 us (0.47); the launches traced: 763 us -> 362 us
  matrix products: 221 us -> 0.86 us
  waiting for transfers between devices: 152 us -> 0 us
  local copies, waits for them, and re-layouts: 130 us -> 3.77 us
  Pallas kernels: 0 us -> 94.4 us
  blocking collectives: 210 us -> 257 us
  other arithmetic: 37.5 us -> 5.17 us
  starting transfers between devices: 8.77 us -> 0 us
    all_to_all x0 -> x2, blocking collectives: none -> 257 us  [exchange(): return lax.all_to_all(box, 'wide', 0, 0, tiled=True).reshape(flat.shape)]
    dot_general x18 -> x0, matrix products: 221 us -> none  [the longest x8 97.7 us: inner_sum(): jnp.einsum('an,bn->ab', left_rows, right_rows, preferred_element_type=jnp...]
    psum x2 -> x0, blocking collectives: 210 us -> none  [the longest x1 168 us: per_device(): total_re, total_im = lax.psum((part_re, part_im), 'wide')]
    all_to_all x2 -> x0, waiting for transfers between devices: 152 us -> none  [the longest x1 152 us: send_out_one(): lax.all_to_all(field, 'wide', split_axis=4, concat_axis=3, tiled=True)]
    pallas_call x0 -> x5, Pallas kernels: none -> 94.4 us  [the longest x1 27.4 us: per_device(): pl.pallas_call(functools.partial(out_kernel, sizes), grid=(lx,), out_shap...]
    all_to_all x4 -> x0, local copies, waits for them, and re-layouts: 36 us -> none  [the longest x2 18.4 us: send_out_one(): lax.all_to_all(field, 'wide', split_axis=4, concat_axis=3, tiled=True)]
    unnamed x66 -> x6, local copies, waits for them, and re-layouts: 35.7 us -> 0.38 us
    transpose x3 -> x1, local copies, waits for them, and re-layouts: 22.8 us -> 0.1 us  [per_device(): gram = jnp.concatenate([jnp.concatenate([gram_a, gram_q], axis=1), jnp.co...]
  transfers between devices with their start and end apart: 2 -> 0, of which waited for: 1 -> 0; matrix products, arithmetic and copies ran while one was open for 1% -> 0% of each run, Pallas kernels for 0% -> 0%
where the time goes in v1:
time: 362 us
  blocking collectives  257 us (71%)
  Pallas kernels  94.4 us (26%)
  other arithmetic  5.17 us (1%)
  local copies, waits for them, and re-layouts  3.77 us (1%)
    all_to_all x2, blocking collectives, exchange(): return lax.all_to_all(box, 'wide', 0, 0, tiled=True).reshape(flat.shape)  257 us
    pallas_call x1, Pallas kernels, per_device(): pl.pallas_call(functools.partial(out_kernel, sizes), grid=(lx,), out_shap...  27.4 us
    pallas_call x1, Pallas kernels, per_device(): pl.pallas_call(functools.partial(mid_kernel, sizes), grid=(ly,), out_shap...  22.9 us
    pallas_call x1, Pallas kernels, per_device(): pl.pallas_call(functools.partial(home_kernel, sizes), grid=(lx,), out_sha...  20 us
    pallas_call x1, Pallas kernels, sum_small(): pl.pallas_call(functools.partial(sum_kernel, n), out_shape=jax.ShapeDtype...  13.6 us
    pallas_call x1, Pallas kernels, per_device(): pl.pallas_call(functools.partial(gram_kernel, kept), grid=(lx,), out_shap...  10.3 us

profile of v1, /device:TPU:0, one launch (start us, length us, event | category | flops | bytes accessed | tf_op | source)
XLA Modules:
  0.0 361.6 jit_solution(11166416285982402535)
XLA Ops:
  0.6 10.3 %shard_map.140.x_ref = f32[16,128]{1,0:T(8,128)} custom-call(bf16[4,2,3,6,192,192]{5,4,3,2,1,0:T(8,128)(2,1)} %locked_ref.3, bf16[1,2,3,6,192,192]{5,4,3,2,1,0:T(8,128)(2,1)} %trial_ref.3), custom_call_target="tpu_custom_call" | custom-call | tf_op jit(solution)/shard_map/pallas_call | solution.py:378
  11.0 13.6 %shard_map.141 = f32[16,128]{1,0:T(8,128)} custom-call(f32[16,128]{1,0:T(8,128)} %shard_map.140.x_ref), custom_call_target="tpu_custom_call" | custom-call | tf_op jit(solution)/shard_map/pallas_call | solution.py:184
  24.6 0.9 slice_add_fusion
  25.5 0.9 fusion.8
  26.4 0.1 copy.36
  26.5 0.1 copy.41
  26.6 0.1 copy.37
  26.7 0.1 copy.38
  26.8 0.1 copy.39
  26.9 0.1 copy.40
  27.0 0.1 copy.33
  27.1 0.1 maximum_maximum_fusion
  27.2 0.1 copy.34
  27.3 0.7 cholesky.16
  28.0 0.1 select_reduce_fusion
  28.0 0.6 compare_reduce_fusion
  28.7 0.6 fusion
  29.3 0.6 custom-call.8
  30.0 0.2 convolution_bitcast_fusion.1
  30.1 0.7 convolution_bitcast_fusion.coef_ref
  30.8 0.6 dynamic_slice.3.wave_ref
  31.4 0.7 jit_solution_.7.qz_ref
  32.1 0.8 jit_solution_.6.qy_ref
  32.9 27.4 %shard_map.142 = f32[10752,128]{1,0:T(8,128)} custom-call(f32[8]{0:T(128)} %convolution_bitcast_fusion.coef_ref, f32[6]{0:T(128)} %dynamic_slice.3.wave_ref, bf16[4,2,3,6,192,192]{5,4,3,2,1,0:T(8,128)(2,1)} %locked_ref.3, bf16[1,2,3,6,192,192]{5,4,3,2,1,0:T(8,128)(2,1)} %trial_ref.3, f32[192,192]{1,0:T(8,128)} %jit_solution_.6.qy_ref, ...), custom_call_target="tpu_custom_call" | custom-call | tf_op jit(solution)/shard_map/pallas_call | solution.py:422
  60.3 130.1 %all_to_all.10 = f32[32,336,128]{2,1,0:T(8,128)} all-to-all(f32[32,336,128]{2,1,0:T(8,128)} %bitcast.30), channel_id=1, replica_groups=mesh['groups'=1,'wide'=32] {'wide'}, dimensions={0} | all-to-all | bytes 11010048 | tf_op jit(solution)/shard_map/all_to_all | solution.py:353
  190.4 22.9 %shard_map.143 = f32[10752,128]{1,0:T(8,128)} custom-call(f32[10752,128]{1,0:T(8,128)} %bitcast.31, f32[3,6,192,192]{3,2,1,0:T(8,128)} %bitcast.33, f32[3,6,192,192]{3,2,1,0:T(8,128)} %bitcast.34, bf16[2,192,384]{2,1,0:T(8,128)(2,1)} %constant.76.clone.ti_ref, bf16[2,192,384]{2,1,0:T(8,128)(2,1)} %constant.77.clone.tf_ref), custom_call_target="tpu_custom_call" | custom-call | tf_op jit(solution)/shard_map/pallas_call | solution.py:433
  213.3 126.7 %all_to_all.11 = f32[32,336,128]{2,1,0:T(8,128)} all-to-all(f32[32,336,128]{2,1,0:T(8,128)} %bitcast.32), channel_id=1, replica_groups=mesh['groups'=1,'wide'=32] {'wide'}, dimensions={0} | all-to-all | bytes 11010048 | tf_op jit(solution)/shard_map/all_to_all | solution.py:353
  340.0 20.0 %shard_map.144 = (bf16[1,2,3,6,192,192]{5,4,3,2,1,0:T(8,128)(2,1)}, f32[64,128]{1,0:T(8,128)}) custom-call(f32[6]{0:T(128)} %dynamic_slice.3.wave_ref, f32[10752,128]{1,0:T(8,128)} %bitcast.29, f32[192,192]{1,0:T(8,128)} %jit_solution_.6.qy_ref, f32[192,192]{1,0:T(8,128)} %jit_solution_.7.qz_ref, bf16[2,192,384]{2,1,0:T(8,128)(2,1)} %constant.78.clone.ty_ref, ...), custom_call_target="tpu_custom_call" | custom-call | tf_op jit(solution)/shard_map/pallas_call | solution.py:444
  360.0 0.9 reduce_sum.10
  360.9 0.1 reduce_sum.14
  361.0 0.1 reduce_sum.18
  361.1 0.5 multiply_bitcast_fusion
  (5 shorter events, 0.0 us)
Async XLA Ops:
  0.6 30.2 %copy-start = (f32[192]{0:T(256)S(1)}, f32[192]{0:T(256)}, u32[]{:S(2)}) copy-start(f32[192]{0:T(256)} %constant.72.clone) | copy-start | bytes 2308

commit v2 on v1

--- a/solution.py
+++ b/solution.py
@@ -60,7 +60,7 @@
         cos, sin = cos[perm_rows], sin[perm_rows]
     if perm_cols is not None:
         cos, sin = cos[:, perm_cols], sin[:, perm_cols]
-    return np.concatenate([cos, sin], axis=1)
+    return np.concatenate([cos, sin], axis=0)
 
 
 def split(x):
@@ -71,10 +71,6 @@
 
 def dot(a, b):
     return jnp.dot(a, b, preferred_element_type=F32)
-
-
-def dot3(a, b):
-    return dot(a[0], b[0]) + (dot(a[0], b[1]) + dot(a[1], b[0]))
 
 
 def times_i(tiles):
@@ -86,11 +82,21 @@
     return [-t2, mid, t0]
 
 
-def left_dft(table, tiles, turned):
-    rows = jnp.concatenate(
-        [jnp.concatenate(tiles, axis=1), jnp.concatenate(turned, axis=1)], axis=0
-    )
-    return dot3(table, split(rows))
+def left_dft(table, tiles):
+    length = table.shape[1]
+    high, low = split(jnp.concatenate(tiles, axis=1))
+    first = dot(table[...], high)
+    both = first[:2 * length] + (first[2 * length:] + dot(table[:2 * length, :], low))
+    real = [both[:length, t * 128:(t + 1) * 128] for t in range(3)]
+    turned = times_i([both[length:, t * 128:(t + 1) * 128] for t in range(3)])
+    return jnp.concatenate([r + i for r, i in zip(real, turned)], axis=1)
+
+
+def right_dft(rows, high_table, low_table):
+    count = rows.shape[0]
+    high, low = split(rows)
+    first = dot(jnp.concatenate([high, low], axis=0), high_table)
+    return first[:count] + (first[count:] + dot(high, low_table))
 
 
 def gram_kernel(kept, locked_ref, trial_ref, out_ref, acc_ref):
@@ -129,12 +135,6 @@
         out_ref[...] = jnp.concatenate([small, jnp.zeros((16 - fields, 128), F32)], axis=0)
 
 
-def peer_of(me, k, n):
-    if n & (n - 1) == 0:
-        return lax.bitwise_xor(me, k)
-    return lax.rem(me + k, n)
-
-
 def greet(me, n):
     barrier = pltpu.get_barrier_semaphore()
 
@@ -220,11 +220,11 @@
 
     curl_re = [-v for v in cross(imag)]
     curl_im = cross(real)
-    for comp in range(3):
-        out = dot3(split(curl_re[comp]), (tz_ref[0, :grid_len], tz_ref[1, :grid_len]))
-        out += dot3(split(curl_im[comp]), (tz_ref[0, grid_len:], tz_ref[1, grid_len:]))
-        tiles = [out[:, t * 128:(t + 1) * 128] for t in range(3)]
-        out = left_dft((ty_ref[0], ty_ref[1]), tiles, times_i(tiles))
+    lines = right_dft(jnp.concatenate(curl_re, axis=0), tz_ref[0, :grid_len], tz_ref[1, :grid_len])
+    lines += right_dft(jnp.concatenate(curl_im, axis=0), tz_ref[0, grid_len:], tz_ref[1, grid_len:])
+    for comp in range(3):
+        part = lines[comp * grid_len:(comp + 1) * grid_len]
+        out = left_dft(ty_ref, [part[:, t * 128:(t + 1) * 128] for t in range(3)])
         for j in range(ly):
             for t in range(3):
                 at = t * rows + step * (3 * ly) + comp * ly + j
@@ -247,7 +247,7 @@
             tiles.append(
                 jnp.concatenate([x_ref[pl.ds(a, n, stride=3 * rows), :] for a in at], axis=0)
             )
-        out = left_dft((ti_ref[0], ti_ref[1]), tiles, times_i(tiles))
+        out = left_dft(ti_ref, tiles)
         space.append([out[:, t * 128:(t + 1) * 128] for t in range(3)])
 
     def lanes(e):
@@ -271,7 +271,7 @@
         for t in range(3):
             sum_re += space[comp][t] * tiles[t]
             sum_im -= space[comp][t] * turned[t]
-        out = left_dft((tf_ref[0], tf_ref[1]), tiles, turned)
+        out = left_dft(tf_ref, tiles)
         for x in range(lx):
             for t in range(3):
                 at = t * rows + x * (3 * ly) + comp * ly + step
@@ -293,7 +293,7 @@
     qx = wave_ref[step]
     qy = qy_ref[...]
     qz = qz_ref[...]
-    real, imag = [], []
+    lines = []
     for comp in range(3):
         tiles = []
         for t in range(3):
@@ -301,9 +301,10 @@
             tiles.append(
                 jnp.concatenate([x_ref[pl.ds(a, n, stride=3 * rows), :] for a in at], axis=0)
             )
-        out = split(left_dft((ty_ref[0], ty_ref[1]), tiles, times_i(tiles)))
-        real.append(dot3(out, (tz_ref[0], tz_ref[1])))
-        imag.append(dot3(out, (tz_ref[2], tz_ref[3])))
+        lines.append(left_dft(ty_ref, tiles))
+    lines = jnp.concatenate(lines, axis=0)
+    both = [right_dft(lines, tz_ref[2 * p], tz_ref[2 * p + 1]) for p in range(2)]
+    real, imag = [[b[c * grid_len:(c + 1) * grid_len] for c in range(3)] for b in both]
 
     def cross(v):
         return [qy * v[2] - qz * v[1], qz * v[0] - qx * v[2], qx * v[1] - qy * v[0]]
@@ -316,36 +317,6 @@
     def _():
         for p in range(2):
             ray_ref[p * n:(p + 1) * n, :] = x_ref[pl.ds(p * rows + 3 * lx * ly, n, stride=3 * rows), :]
-
-
-def swap_kernel(n, x_ref, o_ref, send, recv, here):
-    me = lax.axis_index("wide")
-    greet(me, n)
-
-    def make(k):
-        peer = peer_of(me, k, n)
-        return pltpu.make_async_remote_copy(
-            src_ref=x_ref.at[peer],
-            dst_ref=o_ref.at[me],
-            send_sem=send.at[k],
-            recv_sem=recv.at[k],
-            device_id={"wide": peer},
-            device_id_type=pl.DeviceIdType.MESH,
-        )
-
-    def go(k, carry):
-        make(k).start()
-        return carry
-
-    def finish(k, carry):
-        make(k).wait()
-        return carry
-
-    lax.fori_loop(1, n, go, 0)
-    own = pltpu.make_async_copy(x_ref.at[me], o_ref.at[me], here)
-    own.start()
-    own.wait()
-    lax.fori_loop(1, n, finish, 0)
 
 
 def exchange(flat, n):
@@ -408,10 +379,10 @@
     order_y = np.arange(grid_len).reshape(n, ly).T.reshape(-1)
     order_x = np.arange(grid_len).reshape(n, lx).T.reshape(-1)
     tz_out = jnp.asarray(split_np(right_table(grid_len, 1.0)))
-    ty_out = jnp.asarray(split_np(left_table(grid_len, 1.0, perm_rows=order_y)))
-    tx_in = jnp.asarray(split_np(left_table(grid_len, 1.0, perm_cols=order_x)))
-    tx_out = jnp.asarray(split_np(left_table(grid_len, -1.0, perm_rows=order_x)))
-    ty_in = jnp.asarray(split_np(left_table(grid_len, -1.0, perm_cols=order_y)))
+    ty_out = jnp.asarray(np.concatenate(split_np(left_table(grid_len, 1.0, perm_rows=order_y))))
+    tx_in = jnp.asarray(np.concatenate(split_np(left_table(grid_len, 1.0, perm_cols=order_x))))
+    tx_out = jnp.asarray(np.concatenate(split_np(left_table(grid_len, -1.0, perm_rows=order_x))))
+    ty_in = jnp.asarray(np.concatenate(split_np(left_table(grid_len, -1.0, perm_cols=order_y))))
     back = right_table_back(grid_len, -1.0)
     tz_in = jnp.asarray(
         np.concatenate([split_np(back[:, :grid_len]), split_np(back[:, grid_len:])])

time: 362 us -> 354 us (0.978)
  Pallas kernels: 94.4 us -> 86.7 us
    pallas_call x1, Pallas kernels: 27.4 us -> 23.6 us  [per_device(): pl.pallas_call(functools.partial(out_kernel, sizes), grid=(lx,), out_shap...]
where the time goes in v2:
time: 354 us
  blocking collectives  257 us (73%)
  Pallas kernels  86.7 us (24%)
  other arithmetic  5.17 us (1%)
  local copies, waits for them, and re-layouts  3.77 us (1%)
    all_to_all x2, blocking collectives, exchange(): return lax.all_to_all(box, 'wide', 0, 0, tiled=True).reshape(flat.shape)  257 us
    pallas_call x1, Pallas kernels, per_device(): pl.pallas_call(functools.partial(out_kernel, sizes), grid=(lx,), out_shap...  23.6 us
    pallas_call x1, Pallas kernels, per_device(): pl.pallas_call(functools.partial(mid_kernel, sizes), grid=(ly,), out_shap...  21.6 us
    pallas_call x1, Pallas kernels, per_device(): pl.pallas_call(functools.partial(home_kernel, sizes), grid=(lx,), out_sha...  17.5 us
    pallas_call x1, Pallas kernels, sum_small(): pl.pallas_call(functools.partial(sum_kernel, n), out_shape=jax.ShapeDtype...  13.6 us
    pallas_call x1, Pallas kernels, per_device(): pl.pallas_call(functools.partial(gram_kernel, kept), grid=(lx,), out_shap...  10.3 us

profile of v2, /device:TPU:0, one launch (start us, length us, event | category | flops | bytes accessed | tf_op | source)
XLA Modules:
  0.0 353.9 jit_solution(9783176465811408074)
XLA Ops:
  0.6 10.3 %shard_map.140.x_ref = f32[16,128]{1,0:T(8,128)} custom-call(bf16[4,2,3,6,192,192]{5,4,3,2,1,0:T(8,128)(2,1)} %locked_ref.3, bf16[1,2,3,6,192,192]{5,4,3,2,1,0:T(8,128)(2,1)} %trial_ref.3), custom_call_target="tpu_custom_call" | custom-call | tf_op jit(solution)/shard_map/pallas_call | solution.py:349
  11.0 13.6 %shard_map.141 = f32[16,128]{1,0:T(8,128)} custom-call(f32[16,128]{1,0:T(8,128)} %shard_map.140.x_ref), custom_call_target="tpu_custom_call" | custom-call | tf_op jit(solution)/shard_map/pallas_call | solution.py:184
  24.6 0.9 slice_add_fusion
  25.5 0.9 fusion.8
  26.4 0.1 copy.36
  26.5 0.1 copy.41
  26.6 0.1 copy.37
  26.7 0.1 copy.38
  26.8 0.1 copy.39
  26.9 0.1 copy.40
  27.0 0.1 copy.33
  27.1 0.1 maximum_maximum_fusion
  27.2 0.1 copy.34
  27.3 0.7 cholesky.16
  28.0 0.1 select_reduce_fusion
  28.0 0.6 compare_reduce_fusion
  28.7 0.6 fusion
  29.3 0.6 custom-call.8
  30.0 0.2 convolution_bitcast_fusion.1
  30.1 0.7 convolution_bitcast_fusion.coef_ref
  30.8 0.6 dynamic_slice.3.wave_ref
  31.4 0.7 jit_solution_.7.qz_ref
  32.1 0.8 jit_solution_.6.qy_ref
  32.9 23.6 %shard_map.142 = f32[10752,128]{1,0:T(8,128)} custom-call(f32[8]{0:T(128)} %convolution_bitcast_fusion.coef_ref, f32[6]{0:T(128)} %dynamic_slice.3.wave_ref, bf16[4,2,3,6,192,192]{5,4,3,2,1,0:T(8,128)(2,1)} %locked_ref.3, bf16[1,2,3,6,192,192]{5,4,3,2,1,0:T(8,128)(2,1)} %trial_ref.3, f32[192,192]{1,0:T(8,128)} %jit_solution_.6.qy_ref, ...), custom_call_target="tpu_custom_call" | custom-call | tf_op jit(solution)/shard_map/pallas_call | solution.py:393
  56.4 130.1 %all_to_all.10 = f32[32,336,128]{2,1,0:T(8,128)} all-to-all(f32[32,336,128]{2,1,0:T(8,128)} %bitcast.30), channel_id=1, replica_groups=mesh['groups'=1,'wide'=32] {'wide'}, dimensions={0} | all-to-all | bytes 11010048 | tf_op jit(solution)/shard_map/all_to_all | solution.py:324
  186.5 21.6 %shard_map.143 = f32[10752,128]{1,0:T(8,128)} custom-call(f32[10752,128]{1,0:T(8,128)} %bitcast.31, f32[3,6,192,192]{3,2,1,0:T(8,128)} %bitcast.33, f32[3,6,192,192]{3,2,1,0:T(8,128)} %bitcast.34, bf16[768,192]{1,0:T(8,128)(2,1)} %constant.76.clone.ti_ref, bf16[768,192]{1,0:T(8,128)(2,1)} %constant.77.clone.tf_ref), custom_call_target="tpu_custom_call" | custom-call | tf_op jit(solution)/shard_map/pallas_call | solution.py:404
  208.1 126.7 %all_to_all.11 = f32[32,336,128]{2,1,0:T(8,128)} all-to-all(f32[32,336,128]{2,1,0:T(8,128)} %bitcast.32), channel_id=1, replica_groups=mesh['groups'=1,'wide'=32] {'wide'}, dimensions={0} | all-to-all | bytes 11010048 | tf_op jit(solution)/shard_map/all_to_all | solution.py:324
  334.8 17.5 %shard_map.144 = (bf16[1,2,3,6,192,192]{5,4,3,2,1,0:T(8,128)(2,1)}, f32[64,128]{1,0:T(8,128)}) custom-call(f32[6]{0:T(128)} %dynamic_slice.3.wave_ref, f32[10752,128]{1,0:T(8,128)} %bitcast.29, f32[192,192]{1,0:T(8,128)} %jit_solution_.6.qy_ref, f32[192,192]{1,0:T(8,128)} %jit_solution_.7.qz_ref, bf16[768,192]{1,0:T(8,128)(2,1)} %constant.78.clone.ty_ref, ...), custom_call_target="tpu_custom_call" | custom-call | tf_op jit(solution)/shard_map/pallas_call | solution.py:415
  352.3 0.9 reduce_sum.10
  353.2 0.1 reduce_sum.14
  353.3 0.1 reduce_sum.18
  353.4 0.5 multiply_bitcast_fusion
  (5 shorter events, 0.0 us)
Async XLA Ops:
  0.6 30.2 %copy-start = (f32[192]{0:T(256)S(1)}, f32[192]{0:T(256)}, u32[]{:S(2)}) copy-start(f32[192]{0:T(256)} %constant.72.clone) | copy-start | bytes 2308
